TPU v7x, 32 devices: a whole 2x2x4 slice. The times are simulated.
32 devices in a mesh: space: 16 (over z, y, x), sub: 2 (over core).
Axes of the slice: x: 2, y: 2, z: 4, core: 2. Of those that a mesh axis runs over, the one named last changes fastest.
Arguments:
- fluid_state: float32 [8, 65536], P(None, 'space'), may hold values from 0 to 1
- sphere_state: float32 [7, 65536], P(None, 'space'), may hold values from 0 to 1
- sphere_offset: float32 [3, 65536], P(None, 'space'), may hold values from -1 to 1
- tile_list: int32 [4096, 2], P(('space', 'sub')), may hold values from 0 to 31, as said below
- tile_count: int32 [32], P(('space', 'sub')), may hold values from 32 to 128, as said below
- clump_ids: int32 [65536], P('space'), may hold values from 0 to 127, as said below
- clump_state: float32 [6, 2048], P(None, 'space'), may hold values from -6 to 6
- clump_inverse: float32 [4, 2048], P(None, 'space'), may hold values from 0.02 to 0.2
Outputs:
- clump_velocity: float32 [6, 2048], P(None, 'space')
- sphere_velocity: float32 [3, 65536], P(None, 'space')
Inputs may be any that keep to these rules, and one draw needn't show every extreme that they name: `tile_list`: within a domain the 256 slots of its two devices name distinct pairs; the first entry is below 32, the second below 32. `tile_count`: some device's list is full in every draw. `clump_ids`: among the spheres sent to one owner from all domains, each clump id names exactly 32 spheres.
All inputs are finite; a program needn't handle non-finite values.
Results may differ from a plain program's by a relative error of at most 0.0003.
Values sent between devices are 32-bit elements; how exact they have to be, the bound alone decides.
No kernel may reach another device: no remote copies, remote signals or barrier semaphores. Data moves between devices by JAX's collectives and lax.ppermute only.
A program may use at most 64 MiB of HBM per device.

v0:
```python
import math

import jax
import jax.numpy as jnp
from jax import lax
from jax.sharding import PartitionSpec as P

TILE = 128


support_radius = 0.5
press_coef = 4.0
visc_coef = 1.0
gravity_step = 0.1


def cross_rows(left, right):
    return jnp.stack(
        [
            left[1] * right[2] - left[2] * right[1],
            left[2] * right[0] - left[0] * right[2],
            left[0] * right[1] - left[1] * right[0],
        ],
        axis=0,
    )


def tile_force(fluid_state, sphere_state, sphere_tile, fluid_tile, tile_width):
    spheres = lax.dynamic_slice_in_dim(sphere_state, sphere_tile * tile_width, tile_width, 1)
    fluid = lax.dynamic_slice_in_dim(fluid_state, fluid_tile * tile_width, tile_width, 1)
    separation = spheres[0:3, :, None] - fluid[0:3, None, :]
    distance = jnp.sqrt(jnp.sum(separation * separation, axis=0))
    falloff = jnp.maximum(1.0 - distance / support_radius, 0.0)
    weight = falloff * falloff * falloff * fluid[7][None, :]
    pressure = press_coef * (spheres[6][:, None] + fluid[6][None, :]) * weight
    repulsion = jnp.sum(pressure[None, :, :] * separation, axis=2)
    drag = jnp.sum(weight[None, :, :] * (fluid[3:6, None, :] - spheres[3:6, :, None]), axis=2)
    return repulsion + visc_coef * drag


def add_tile(forces, fluid_state, sphere_state, pair, tile_width):
    term = tile_force(fluid_state, sphere_state, pair[0], pair[1], tile_width)
    first_col = pair[0] * tile_width
    current = lax.dynamic_slice_in_dim(forces, first_col, tile_width, 1)
    return lax.dynamic_update_slice_in_dim(forces, current + term, first_col, 1)


def clump_totals(sphere_loads, owned_ids, clump_count):
    total_rows = sphere_loads.shape[1]
    block_rows = math.gcd(total_rows, 2048)
    columns = jnp.arange(clump_count, dtype=jnp.int32)

    def accumulate(block_number, totals):
        first_row = block_number * block_rows
        row_block = lax.dynamic_slice_in_dim(sphere_loads, first_row, block_rows, 1)
        labels = lax.dynamic_slice_in_dim(owned_ids, first_row, block_rows, 0)
        one_hot = (labels[:, None] == columns[None, :]).astype(jnp.float32)
        return totals + jnp.dot(
            row_block, one_hot, precision=lax.Precision.HIGHEST, preferred_element_type=jnp.float32
        )

    return lax.fori_loop(
        0, total_rows // block_rows, accumulate, jnp.zeros((6, clump_count), jnp.float32)
    )


def rigid_update(totals, clump_state, clump_inverse):
    gravity_pull = jnp.array([0.0, 0.0, -gravity_step], jnp.float32)[:, None]
    linear = clump_state[0:3] + clump_inverse[0:1] * totals[0:3] + gravity_pull
    angular = clump_state[3:6] + clump_inverse[1:4] * totals[3:6]
    return jnp.concatenate([linear, angular], axis=0)


def send_loads(forces, offsets, labels):
    rows = forces.shape[1] * forces.shape[2]
    loads = jnp.concatenate([forces, cross_rows(offsets, forces)], axis=0)
    arrived, arrived_ids = (
        lax.all_to_all(loads, "space", split_axis=1, concat_axis=1, tiled=True),
        lax.all_to_all(labels, "space", split_axis=1, concat_axis=1, tiled=True),
    )
    return (arrived.reshape(6, rows), arrived_ids.reshape(rows), None)


def send_back(velocity, arrived_ids, offsets):
    owner_count = offsets.shape[1]
    per_owner = offsets.shape[2]
    picked = jnp.take(velocity, arrived_ids, axis=1)
    returned = lax.all_to_all(
        picked.reshape(6, owner_count, per_owner), "space", split_axis=1, concat_axis=1, tiled=True
    )
    return returned[0:3] + cross_rows(returned[3:6], offsets)


def per_device(
    fluid_state,
    sphere_state,
    sphere_offset,
    tile_list,
    tile_count,
    clump_ids,
    clump_state,
    clump_inverse,
):
    tile_width = TILE
    spheres_here = sphere_state.shape[1]
    owner_count = lax.axis_size("space")
    slot_count = spheres_here // owner_count
    clump_count = clump_state.shape[1]
    forces = jnp.zeros((3, spheres_here), jnp.float32)

    def own_step(entry_number, forces):
        return add_tile(forces, fluid_state, sphere_state, tile_list[entry_number], tile_width)

    forces = lax.fori_loop(0, tile_count[0], own_step, forces)
    summed = lax.psum(forces, "sub")
    offsets = sphere_offset.reshape(3, owner_count, slot_count)
    labels = clump_ids.reshape(1, owner_count, slot_count)
    arrived, arrived_ids, arrived_offsets = send_loads(
        summed.reshape(3, owner_count, slot_count), offsets, labels
    )
    totals = clump_totals(arrived, arrived_ids, clump_count)
    velocity = rigid_update(totals, clump_state, clump_inverse)
    sphere_velocity = send_back(velocity, arrived_ids, offsets).reshape(3, spheres_here)
    return (velocity, sphere_velocity)


def solution(mesh):
    in_specs = (
        P(None, "space"),
        P(None, "space"),
        P(None, "space"),
        P(("space", "sub"), None),
        P(("space", "sub")),
        P("space"),
        P(None, "space"),
        P(None, "space"),
    )
    out_specs = (P(None, "space"), P(None, "space"))
    return jax.shard_map(
        per_device, mesh=mesh, in_specs=in_specs, out_specs=out_specs, check_vma=False
    )
```

profile of v0, /device:TPU:0, one launch (start us, length us, event | category | flops | bytes accessed | tf_op | source)
XLA Modules:
  0.0 722.4 jit_solution(8726849328422224505)
XLA Ops:
  0.6 8.3 %all-to-all-start.1 = ((s32[1,16,256]{2,0,1:T(1,128)}), s32[1,16,256]{2,0,1:T(1,128)S(1)}, u32[]{:S(2)}, u32[]{:S(2)}) async-start(s32[1,16,256]{2,0,1:T(1,128)} %bitcast.67), calls=%async_computation.1 | async-start | bytes 32768 | tf_op jit(solution)/shard_map/all_to_all | solution.py:79
  9.6 1.0 fusion.12
  10.7 173.2 %while.24 = (s32[]{:T(128)}, f32[3,4096]{1,0:T(4,128)S(1)}, s32[]{:T(128)}, s32[128,2]{0,1:T(2,128)}, f32[7,4096]{1,0:T(8,128)}, /*index=5*/f32[8,4096]{1,0:T(8,...) while((s32[]{:T(128)}, f32[3,4096]{1,0:T(4,128)S(1)}, s32[]{:T(128)}, ...), condition=%wide.region_4.0_spmd, body=%wide.region_0.0_spmd.sunk | while | flops 573453 | bytes 446243 | solution.py:114
  11.3 0.8 constant_dynamic-slice_fusion.6
  16.6 0.8 constant_dynamic-slice_fusion.6
  21.8 0.8 constant_dynamic-slice_fusion.6
  27.0 0.8 constant_dynamic-slice_fusion.6
  37.5 0.8 constant_dynamic-slice_fusion.6
  42.7 0.8 constant_dynamic-slice_fusion.6
  47.9 0.8 constant_dynamic-slice_fusion.6
  53.2 0.8 constant_dynamic-slice_fusion.6
  63.6 0.8 constant_dynamic-slice_fusion.6
  68.8 0.8 constant_dynamic-slice_fusion.6
  74.1 0.8 constant_dynamic-slice_fusion.6
  79.3 0.8 constant_dynamic-slice_fusion.6
  84.5 0.8 constant_dynamic-slice_fusion.6
  89.7 0.8 constant_dynamic-slice_fusion.6
  100.2 0.8 constant_dynamic-slice_fusion.6
  105.4 0.8 constant_dynamic-slice_fusion.6
  110.7 0.8 constant_dynamic-slice_fusion.6
  115.9 0.8 constant_dynamic-slice_fusion.6
  121.1 0.8 constant_dynamic-slice_fusion.6
  126.3 0.8 constant_dynamic-slice_fusion.6
  136.8 0.8 constant_dynamic-slice_fusion.6
  142.0 0.8 constant_dynamic-slice_fusion.6
  147.2 0.8 constant_dynamic-slice_fusion.6
  183.9 50.1 %psum.7 = f32[3,4096]{1,0:T(4,128)S(1)} all-reduce(f32[3,4096]{1,0:T(4,128)S(1)} %get-tuple-element.129), channel_id=1, replica_groups=mesh['space'=16,'sub'=2] {'sub'}, use_global_device_ids=true, to_apply=%region_5.0 | all-reduce | flops 12288 | bytes 98304 | tf_op jit(solution)/shard_map/psum | solution.py:115
  234.8 455.3 %all-to-all-start = ((f32[6,16,256]{2,0,1:T(8,128)}), f32[6,16,256]{2,0,1:T(8,128)S(1)}, u32[]{:S(2)}, u32[]{:S(2)}) async-start(f32[6,16,256]{2,0,1:T(8,128)} %pad_maximum_fusion), calls=%async_computation | async-start | bytes 262144 | tf_op jit(solution)/shard_map/all_to_all | solution.py:78
  690.1 7.9 %all-to-all-done = f32[6,16,256]{2,0,1:T(8,128)S(1)} async-done(((f32[6,16,256]{2,0,1:T(8,128)}), f32[6,16,256]{2,0,1:T(8,128)S(1)}, u32[]{:S(2)}, u32[]{:S(2)}) %all-to-all-start) | async-done | bytes 98336 | tf_op jit(solution)/shard_map/all_to_all | solution.py:78
  698.0 1.2 while.25
  699.5 10.8 %gather_fusion = f32[4096,6]{1,0:T(8,128)S(1)} fusion(f32[6,128]{0,1:T(8,128)S(1)} %copy.29, s32[4096]{0:T(1024)S(1)} %broadcast_clamp_fusion), kind=kCustom, calls=%fused_computation | custom fusion | bytes 212992 | tf_op jit(solution)/shard_map/jit(_take)/gather | solution.py:87
  710.9 10.8 %all_to_all.15 = f32[6,16,256]{2,0,1:T(8,128)S(1)} all-to-all(f32[6,16,256]{2,0,1:T(8,128)S(1)} %broadcast_select_fusion), channel_id=1, replica_groups=mesh['space'=16,'sub'=2] {'space'}, dimensions={1} | all-to-all | bytes 196608 | tf_op jit(solution)/shard_map/all_to_all | solution.py:88
  (402 shorter events, 94.5 us)
Async XLA Ops:
  0.6 234.2 %all-to-all-start.1 = ((s32[1,16,256]{2,0,1:T(1,128)}), s32[1,16,256]{2,0,1:T(1,128)S(1)}, u32[]{:S(2)}, u32[]{:S(2)}) async-start(s32[1,16,256]{2,0,1:T(1,128)} %bitcast.67), calls=%async_computation.1 | async-start | bytes 32768 | tf_op jit(solution)/shard_map/all_to_all | solution.py:79
  183.8 515.4 %copy-start.1 = (f32[6,128]{1,0:T(8,128)S(1)}, f32[6,128]{1,0:T(8,128)}, u32[]{:S(2)}) copy-start(f32[6,128]{1,0:T(8,128)} %param.19) | copy-start | bytes 9220
  183.8 515.4 %copy-start.2 = (f32[4,128]{1,0:T(4,128)S(1)}, f32[4,128]{1,0:T(4,128)}, u32[]{:S(2)}) copy-start(f32[4,128]{1,0:T(4,128)} %param.20) | copy-start | bytes 6148
  183.9 515.4 %copy-start.3 = (f32[3]{0:T(128)S(1)}, f32[3]{0:T(128)}, u32[]{:S(2)}) copy-start(f32[3]{0:T(128)} %constant.71.clone) | copy-start | bytes 40
  234.8 463.2 %all-to-all-start = ((f32[6,16,256]{2,0,1:T(8,128)}), f32[6,16,256]{2,0,1:T(8,128)S(1)}, u32[]{:S(2)}, u32[]{:S(2)}) async-start(f32[6,16,256]{2,0,1:T(8,128)} %pad_maximum_fusion), calls=%async_computation | async-start | bytes 262144 | tf_op jit(solution)/shard_map/all_to_all | solution.py:78
  699.3 23.1 %copy-start = (f32[6,128]{1,0:T(8,128)}, f32[6,128]{1,0:T(8,128)S(1)}, u32[]{:S(2)}) copy-start(f32[6,128]{1,0:T(8,128)S(1)} %pad_maximum_fusion.1) | copy-start | bytes 9220
where the time goes:
time: 736 us; the launch traced here: 722 us
  starting transfers between devices  464 us (63%)
  local copies, waits for them, and re-layouts  103 us (14%)
  loops' own time  65.6 us (9%)
  blocking collectives  60.9 us (8%)
  other arithmetic  19.4 us (3%)
  waiting for transfers between devices  7.88 us (1%)
    all_to_all x1, starting transfers between devices, send_loads(): lax.all_to_all(loads, 'space', split_axis=1, concat_axis=1, tiled=True)  455 us
    another operation x1, loops' own time, per_device(): forces = lax.fori_loop(0, tile_count[0], own_step, forces)  65.6 us
    psum x1, blocking collectives, per_device(): summed = lax.psum(forces, 'sub')  50.1 us
    dynamic_slice x33, local copies, waits for them, and re-layouts, own_step(): tile_list[entry_number]  24.9 us
    dynamic_slice x33, local copies, waits for them, and re-layouts, tile_force(): lax.dynamic_slice_in_dim(fluid_state, fluid_tile * tile_width, tile_width...  22.9 us
    dynamic_slice x33, local copies, waits for them, and re-layouts, tile_force(): lax.dynamic_slice_in_dim(sphere_state, sphere_tile * tile_width, tile_wid...  22.7 us
    slice x33, local copies, waits for them, and re-layouts, add_tile(): term = tile_force(fluid_state, sphere_state, pair[0], pair[1], tile_width)  18.7 us
  transfers between devices with their start and end apart: 2, of which 1 were waited for; matrix products, arithmetic and copies ran while one was open for 15% of the time, Pallas kernels for 0%

commit v1 on v0

v1 whole, which is shorter than its diff:
```python
import functools
import math

import jax
import jax.numpy as jnp
from jax import lax
from jax.experimental import pallas as pl
from jax.experimental.pallas import tpu as pltpu
from jax.sharding import PartitionSpec as P

TILE = 128
SLOT = 256
UNROLL = 4

support_radius = 0.5
press_coef = 4.0
visc_coef = 1.0
gravity_step = 0.1

f32 = jnp.float32
bf16 = jnp.bfloat16


def split_two(value):
    high = value.astype(bf16)
    return high, (value - high.astype(f32)).astype(bf16)


def cross(left, right):
    return [
        left[1] * right[2] - left[2] * right[1],
        left[2] * right[0] - left[0] * right[2],
        left[0] * right[1] - left[1] * right[0],
    ]


def group_of(owners):
    return math.gcd(owners, 16)


def loads_kernel(
    count_ref, list_ref, fluid_ref, sphere_ref, offset_ref, ids_ref, out_ref,
    place_ref, wide_ref, terms_ref, weight_ref, acc_ref,
):
    fluid_tiles = fluid_ref.shape[1] // TILE
    spheres = sphere_ref.shape[1]
    clumps = out_ref.shape[1]
    owners = out_ref.shape[0] // 6

    place_ref[...] = sphere_ref[0:3, :] * (1.0 / support_radius) - 1.0
    acc_ref[...] = jnp.zeros_like(acc_ref)
    weight_ref[...] = jnp.zeros_like(weight_ref)

    @pl.loop(0, fluid_tiles)
    def _(tile):
        cols = pl.ds(pl.multiple_of(tile * TILE, TILE), TILE)
        state = fluid_ref[:, cols]
        row = lax.broadcasted_iota(jnp.int32, state.shape, 0)
        state = jnp.where(row < 3, state * (1.0 / support_radius) - 1.0, state)
        mass = state[7:8]
        first = jnp.where(row < 7, state * mass, state)
        second = jnp.where(row < 3, state * (mass * state[6:7]), 0.0)
        high, low = split_two(jnp.concatenate([first, second], axis=0))
        both = jnp.concatenate([high, low], axis=0)
        terms_ref[tile] = jnp.concatenate([both, both], axis=1)
        turned = state.T
        for k in range(3):
            wide_ref[k, cols, :] = jnp.broadcast_to(turned[:, k : k + 1], (TILE, TILE))

    def pair_weights(slot, part):
        a = list_ref[0, slot]
        b = list_ref[1, slot]
        cols = pl.ds(pl.multiple_of(a * TILE, TILE), TILE)
        rows = pl.ds(pl.multiple_of(b * TILE, TILE), TILE)
        dx = place_ref[0:1, cols] - wide_ref[0, rows, :]
        dy = place_ref[1:2, cols] - wide_ref[1, rows, :]
        dz = place_ref[2:3, cols] - wide_ref[2, rows, :]
        square = jnp.maximum(dx * dx + dy * dy + dz * dz, 1e-30)
        falloff = jnp.maximum(1.0 - square * lax.rsqrt(square), 0.0)
        high, low = split_two(falloff * falloff * falloff)
        weight_ref[part, 0:TILE, :] = high
        weight_ref[part, TILE:, :] = low

    def add_sums(slot, part, live):
        a = list_ref[0, slot]
        b = list_ref[1, slot]
        cols = pl.ds(pl.multiple_of(a * TILE, TILE), TILE)
        sums = jnp.dot(terms_ref[b], weight_ref[part], preferred_element_type=f32)
        acc_ref[:, cols] += live * (sums[0:16] + sums[16:32])

    count = count_ref[0]
    trips = (count + UNROLL - 1) // UNROLL

    @pl.loop(0, trips + 1)
    def _(trip):
        for part in range(UNROLL):
            slot = (trip - 1) * UNROLL + part
            live = jnp.where((slot >= 0) & (slot < count), 1.0, 0.0).astype(f32)
            add_sums(jnp.maximum(slot, 0), part, live)
        for part in range(UNROLL):
            slot = jnp.minimum(trip * UNROLL + part, list_ref.shape[1] - 1)
            pair_weights(slot, part)

    group = group_of(owners)
    width = group * SLOT

    @pl.loop(0, owners // group)
    def _(block):
        cols = pl.ds(pl.multiple_of(block * width, width), width)
        acc = acc_ref[:, cols]
        place = place_ref[:, cols]
        sphere = sphere_ref[:, cols]
        offset = offset_ref[:, cols]
        total = acc[7:8]
        pull = total * place - acc[0:3]
        press = acc[6:7] * place - acc[8:11]
        scale = press_coef * support_radius
        force = scale * (sphere[6:7] * pull + press) + visc_coef * (acc[3:6] - total * sphere[3:6])
        force = [force[k : k + 1] for k in range(3)]
        turn = cross([offset[k : k + 1] for k in range(3)], force)
        loads = jnp.concatenate(force + turn + [jnp.zeros_like(force[0])] * 2, axis=0)
        high, low = split_two(loads)
        both = jnp.concatenate([high, low], axis=0)
        column = lax.broadcasted_iota(jnp.int32, (clumps, SLOT), 0)
        results = []
        for k in range(group):
            here = pl.ds(pl.multiple_of(block * width + k * SLOT, SLOT), SLOT)
            one_hot = jnp.where(column == ids_ref[:, here], 1.0, 0.0).astype(bf16)
            sums = lax.dot_general(
                both[:, k * SLOT : (k + 1) * SLOT], one_hot, (((1,), (1,)), ((), ())),
                preferred_element_type=f32,
            )
            results.append((sums[0:8] + sums[8:16])[0:6])
        start = pl.multiple_of(block * (6 * group), math.gcd(6 * group, 8))
        out_ref[pl.ds(start, 6 * group), :] = jnp.concatenate(results, axis=0)


def velocity_kernel(totals_ref, state_ref, inverse_ref, offset_ref, ids_ref, clump_ref, sphere_ref, own_ref):
    owners, _, clumps = state_ref.shape
    group = group_of(owners)
    row = lax.broadcasted_iota(jnp.int32, (6, clumps), 0)
    gravity = jnp.where(row == 2, -gravity_step, 0.0)
    me = lax.axis_index("space")

    @pl.loop(0, owners // group)
    def _(block):
        start = pl.multiple_of(block * (6 * group), math.gcd(6 * group, 8))
        totals = totals_ref[pl.ds(start, 6 * group), :]
        for k in range(group):
            owner = block * group + k
            inverse = inverse_ref[owner]
            factor = jnp.concatenate([inverse[0:1]] * 3 + [inverse[1:4]], axis=0)
            velocity = state_ref[owner] + factor * totals[6 * k : 6 * k + 6] + gravity
            own_ref[owner] = velocity
            high, low = split_two(jnp.concatenate([velocity, jnp.zeros((2, clumps), f32)], axis=0))
            both = jnp.concatenate([high, low], axis=0)
            here = pl.ds(pl.multiple_of(owner * SLOT, SLOT), SLOT)
            column = lax.broadcasted_iota(jnp.int32, (clumps, SLOT), 0)
            one_hot = jnp.where(column == ids_ref[:, here], 1.0, 0.0).astype(bf16)
            picked = jnp.dot(both, one_hot, preferred_element_type=f32)
            picked = picked[0:8] + picked[8:16]
            offset = offset_ref[:, here]
            turn = cross([picked[3 + i : 4 + i] for i in range(3)], [offset[i : i + 1] for i in range(3)])
            sphere_ref[:, here] = picked[0:3] + jnp.concatenate(turn, axis=0)

    clump_ref[...] = own_ref[me]


def per_device(
    fluid_state, sphere_state, sphere_offset, tile_list, tile_count, clump_ids, clump_state, clump_inverse
):
    owners = lax.axis_size("space")
    spheres = sphere_state.shape[1]
    fluid = fluid_state.shape[1]
    clumps = clump_state.shape[1]
    ids = clump_ids.reshape(1, spheres)
    vmem = pl.BlockSpec(memory_space=pltpu.VMEM)
    smem = pl.BlockSpec(memory_space=pltpu.SMEM)

    all_state = lax.all_gather(clump_state, "space", axis=0)
    all_inverse = lax.all_gather(clump_inverse, "space", axis=0)

    partial = pl.pallas_call(
        loads_kernel,
        out_shape=jax.ShapeDtypeStruct((owners * 6, clumps), f32),
        in_specs=[smem, smem, vmem, vmem, vmem, vmem],
        out_specs=vmem,
        scratch_shapes=[
            pltpu.VMEM((3, spheres), f32),
            pltpu.VMEM((3, fluid, TILE), f32),
            pltpu.VMEM((fluid // TILE, 32, 2 * TILE), bf16),
            pltpu.VMEM((UNROLL, 2 * TILE, TILE), bf16),
            pltpu.VMEM((16, spheres), f32),
        ],
        compiler_params=pltpu.CompilerParams(vmem_limit_bytes=48 * 1024 * 1024),
        name="clump_loads",
    )(tile_count, tile_list.T, fluid_state, sphere_state, sphere_offset, ids)

    totals = lax.psum(partial, ("space", "sub"))

    velocity, sphere_velocity = pl.pallas_call(
        velocity_kernel,
        out_shape=(
            jax.ShapeDtypeStruct((6, clumps), f32),
            jax.ShapeDtypeStruct((3, spheres), f32),
        ),
        in_specs=[vmem] * 5,
        out_specs=(vmem, vmem),
        scratch_shapes=[pltpu.VMEM((owners, 6, clumps), f32)],
        compiler_params=pltpu.CompilerParams(vmem_limit_bytes=48 * 1024 * 1024),
        name="velocities",
    )(totals, all_state, all_inverse, sphere_offset, ids)
    return velocity, sphere_velocity


def solution(mesh):
    in_specs = (
        P(None, "space"),
        P(None, "space"),
        P(None, "space"),
        P(("space", "sub"), None),
        P(("space", "sub")),
        P("space"),
        P(None, "space"),
        P(None, "space"),
    )
    out_specs = (P(None, "space"), P(None, "space"))
    return jax.shard_map(
        per_device, mesh=mesh, in_specs=in_specs, out_specs=out_specs, check_vma=False
    )
```

time: 736 us -> 137 us (0.19); the launches traced: 722 us -> 137 us
  starting transfers between devices: 464 us -> 0 us
  local copies, waits for them, and re-layouts: 103 us -> 3.35 us
  loops' own time: 65.6 us -> 0 us
  blocking collectives: 60.9 us -> 119 us
  other arithmetic: 19.4 us -> 0 us
  Pallas kernels: 0 us -> 12.7 us
  waiting for transfers between devices: 7.88 us -> 0 us
    all_to_all x2 -> x0, starting transfers between devices: 464 us -> none  [the longest x1 455 us: send_loads(): lax.all_to_all(loads, 'space', split_axis=1, concat_axis=1, tiled=True)]
    all_gather x0 -> x2, blocking collectives: none -> 81.9 us  [the longest x1 42.7 us: per_device(): all_inverse = lax.all_gather(clump_inverse, 'space', axis=0)]
    dynamic_slice x101 -> x0, local copies, waits for them, and re-layouts: 70.5 us -> none  [the longest x33 24.9 us: own_step(): tile_list[entry_number]]
    another operation x2 -> x0, loops' own time: 65.6 us -> none  [the longest x1 65.6 us: per_device(): forces = lax.fori_loop(0, tile_count[0], own_step, forces)]
    slice x134 -> x0, local copies, waits for them, and re-layouts: 20.2 us -> none  [the longest x33 18.7 us: add_tile(): term = tile_force(fluid_state, sphere_state, pair[0], pair[1], tile_width)]
    reduce_sum x66 -> x0, other arithmetic: 14.2 us -> none  [the longest x33 10.5 us: tile_force(): repulsion = jnp.sum(pressure[None, :, :] * separation, axis=2)]
    psum x1, blocking collectives: 50.1 us -> 37.3 us  [per_device(): totals = lax.psum(partial, ('space', 'sub'))]
    pallas_call x0 -> x2, Pallas kernels: none -> 12.7 us  [the longest x1 11.7 us: per_device(): pl.pallas_call(loads_kernel, out_shape=jax.ShapeDtypeStruct((owners * 6,...]
  transfers between devices with their start and end apart: 2 -> 0, of which waited for: 1 -> 0; matrix products, arithmetic and copies ran while one was open for 15% -> 0% of each run, Pallas kernels for 0% -> 0%
where the time goes in v1:
time: 137 us
  blocking collectives  119 us (87%)
  Pallas kernels  12.7 us (9%)
  local copies, waits for them, and re-layouts  3.35 us (2%)
    all_gather x1, blocking collectives, per_device(): all_inverse = lax.all_gather(clump_inverse, 'space', axis=0)  42.7 us
    all_gather x1, blocking collectives, per_device(): all_state = lax.all_gather(clump_state, 'space', axis=0)  39.2 us
    psum x1, blocking collectives, per_device(): totals = lax.psum(partial, ('space', 'sub'))  37.3 us
    pallas_call x1, Pallas kernels, per_device(): pl.pallas_call(loads_kernel, out_shape=jax.ShapeDtypeStruct((owners * 6,...  11.7 us
    unnamed x16, local copies, waits for them, and re-layouts  3.35 us

profile of v1, /device:TPU:0, one launch (start us, length us, event | category | flops | bytes accessed | tf_op | source)
XLA Modules:
  0.0 136.5 jit_solution(87018368409976104)
XLA Ops:
  1.3 0.0 copy-start.7
  1.3 0.7 copy-done.7
  2.0 0.0 copy-start.4
  2.0 0.0 copy-start.5
  2.0 42.7 %all-gather.3.inverse_ref = f32[16,4,128]{2,1,0:T(4,128)S(1)} all-gather(f32[1,4,128]{2,1,0:T(4,128)S(1)} %bitcast.8), channel_id=3, replica_groups=mesh['space'=16,'sub'=2] {'space'}, dimensions={0}, use_global_device_ids=true | all-gather | bytes 34816 | tf_op jit(solution)/shard_map/all_gather | solution.py:181
  44.6 0.0 copy-done.4
  44.6 0.0 copy-done.5
  44.6 0.0 copy-start
  44.6 0.8 copy-done
  45.5 0.0 copy-start.2
  45.5 0.9 copy-done.2
  46.4 0.0 copy-start.3
  46.4 0.9 copy-done.3
  47.3 11.7 %clump_loads.1 = f32[96,128]{1,0:T(8,128)S(1)} custom-call(s32[1]{0:T(128)S(6)} %copy.10.count_ref, s32[2,128]{1,0:T(2,128)S(1)} %bitcast.6, f32[8,4096]{1,0:T(8,128)S(1)} %copy-done.2, f32[7,4096]{1,0:T(8,128)S(1)} %copy-done.3, f32[3,4096]{1,0:T(4,128)S(1)} %copy-done, s32[1,4096]{1,0:T(1,128)S(1)} %bitcast.4), custom_call_target="tpu_custom_call" | custom-call | tf_op jit(solution)/shard_map/clump_loads/pallas_call | solution.py:183
  59.0 0.0 copy-start.6
  59.0 0.0 copy-start.1
  59.0 37.3 %psum.7.totals_ref = f32[96,128]{1,0:T(8,128)S(1)} all-reduce(f32[96,128]{1,0:T(8,128)S(1)} %clump_loads.1), channel_id=1, replica_groups=mesh['space'=16,'sub'=2] {'space','sub'}, use_global_device_ids=true, to_apply=%region_0.0 | all-reduce | flops 12288 | bytes 98304 | tf_op jit(solution)/shard_map/psum | solution.py:199
  96.3 0.0 copy-done.6
  96.3 39.2 %all-gather.2.state_ref = f32[16,6,128]{2,1,0:T(8,128)S(1)} all-gather(f32[1,6,128]{2,1,0:T(8,128)S(1)} %bitcast.7), channel_id=2, replica_groups=mesh['space'=16,'sub'=2] {'space'}, dimensions={0}, use_global_device_ids=true | all-gather | bytes 52224 | tf_op jit(solution)/shard_map/all_gather | solution.py:180
  135.6 0.0 copy-done.1
  135.6 1.0 velocities.1
Async XLA Ops:
  1.3 0.7 copy-start.7
  2.0 42.7 %copy-start.4 = (s32[4096]{0:T(1024)S(1)}, s32[4096]{0:T(1024)}, u32[]{:S(2)}) copy-start(s32[4096]{0:T(1024)} %param.13) | copy-start | bytes 49156
  2.0 42.7 %copy-start.5 = (s32[128,2]{0,1:T(2,128)S(1)}, s32[128,2]{0,1:T(2,128)}, u32[]{:S(2)}) copy-start(s32[128,2]{0,1:T(2,128)} %param.11) | copy-start | bytes 3076
  44.6 0.8 copy-start
  45.5 0.9 copy-start.2
  46.4 0.9 copy-start.3
  59.0 37.3 %copy-start.6 = (f32[6,128]{1,0:T(8,128)S(1)}, f32[6,128]{1,0:T(8,128)}, u32[]{:S(2)}) copy-start(f32[6,128]{1,0:T(8,128)} %param.14) | copy-start | bytes 9220
  59.0 76.6 %copy-start.1 = (f32[3,4096]{1,0:T(4,128)S(1)}, f32[3,4096]{1,0:T(4,128)}, u32[]{:S(2)}) copy-start(f32[3,4096]{1,0:T(4,128)} %offset_ref.3) | copy-start | bytes 147460
